TPU v7x, 32 devices: a whole 2x2x4 slice. The times are simulated.
32 devices in a mesh: hours: 2 (over x), chan: 2 (over core), freq: 8 (over z, y).
Axes of the slice: x: 2, y: 2, z: 4, core: 2. Of those that a mesh axis runs over, the one named last changes fastest.
Arguments:
- samples: bfloat16 [1152, 32, 1024], P('chan', ('hours', 'freq')), parts along dimension 1, may hold values from -18 to 18
Outputs:
- cross_spectra: bfloat16 [2, 256, 1152, 1152], P(None, ('hours', 'freq'), None, 'chan'), parts along dimension 1
There are 2 independent parts, one for each index of `hours`. A program takes and returns all parts, laid end to end along the dimension named above; each array names one. Nothing has to cross between parts.
All inputs are finite; a program needn't handle non-finite values.
Results may differ from a plain program's by a relative error of at most 0.008.
Values may be sent and summed in bfloat16 or wider, within the bound.
A program may use at most 192 MiB of HBM per device.

v0:
```python
import math
import jax
import jax.numpy as jnp
from jax import lax
from jax.sharding import PartitionSpec as P

BINS = 128


def padded_2(cells, sides, width):
    for axis, dim in sides:
        count = lax.axis_size(axis)
        ends = count - 1
        head = lax.slice_in_dim(cells, 0, width, axis=dim)
        tail = lax.slice_in_dim(cells, cells.shape[dim] - width, cells.shape[dim], axis=dim)
        cells = jnp.concatenate(
            [
                lax.ppermute(tail, axis, [(i, (i + 1) % count) for i in range(ends)]),
                cells,
                lax.ppermute(head, axis, [((i + 1) % count, i) for i in range(ends)]),
            ],
            axis=dim,
        )
    return cells


def from_behind(value, axis, steps):
    count = lax.axis_size(axis)
    pairs = [(source, (source + steps) % count) for source in range(count)]
    return lax.ppermute(value, axis, pairs)


def bin_table(length, bins):
    position = lax.broadcasted_iota(jnp.int32, (length, bins), 0)
    number = lax.broadcasted_iota(jnp.int32, (length, bins), 1) + 1
    phase = (position * number % length).astype(jnp.float32) * (2.0 * math.pi / length)
    taper = 0.5 - 0.5 * jnp.cos(position.astype(jnp.float32) * (2.0 * math.pi / length))
    factor = math.sqrt(8.0 / (3.0 * length))
    table = jnp.concatenate([taper * jnp.cos(phase), -(taper * jnp.sin(phase))], axis=1) * factor
    return table.astype(jnp.bfloat16)


def whiten(padded, first_bin, total_bins):
    count_bins = padded.shape[1] - 4
    values = padded.astype(jnp.float32)
    power = values[0] * values[0] + values[1] * values[1]
    summed = power[0:count_bins] + power[1 : count_bins + 1]
    summed = summed + power[2 : count_bins + 2]
    summed = summed + power[3 : count_bins + 3]
    summed = summed + power[4 : count_bins + 4]
    which = first_bin + jnp.arange(count_bins, dtype=jnp.int32)
    upper = jnp.minimum(which + 2, total_bins - 1)
    lower = jnp.maximum(which - 2, 0)
    count = (upper - lower + 1).astype(jnp.float32)
    level = jnp.maximum(summed / count[:, None, None], 0.1)
    return (values[:, 2 : count_bins + 2] / jnp.sqrt(level)[None]).astype(jnp.bfloat16)


def local(samples):
    local_channels, local_windows, length = samples.shape
    table = bin_table(length, BINS)
    spectrum = jnp.einsum("cws,sj->jwc", samples, table, preferred_element_type=jnp.float32)
    spectrum = spectrum.reshape(2, BINS, local_windows, local_channels).astype(jnp.bfloat16)
    arrived = lax.all_to_all(spectrum, "freq", split_axis=1, concat_axis=2, tiled=True)
    rimmed = padded_2(arrived, (("freq", 1),), 2)
    whitened = whiten(rimmed, lax.axis_index("freq") * arrived.shape[1], BINS)
    local_bins = whitened.shape[1]
    windows = whitened.shape[2]
    blocks = lax.axis_size("chan")
    own_block = lax.axis_index("chan")
    scale = 1.0 / windows
    visitors = [whitened]
    visiting = whitened
    visiting = from_behind(visiting, "chan", 1)
    visitors.append(visiting)
    stacked = jnp.stack(visitors)
    order = (own_block - jnp.arange(blocks, dtype=jnp.int32)) % blocks
    ordered = jnp.take(stacked, order, axis=0)
    every = jnp.transpose(ordered, (1, 2, 3, 0, 4)).reshape(
        2, local_bins, windows, blocks * local_channels
    )
    real_part = jnp.einsum("pkwb,pkwa->kba", every, whitened, preferred_element_type=jnp.float32)
    imag_part = jnp.einsum(
        "kwb,kwa->kba", every[0], whitened[1], preferred_element_type=jnp.float32
    )
    imag_part = imag_part - jnp.einsum(
        "kwb,kwa->kba", every[1], whitened[0], preferred_element_type=jnp.float32
    )
    return (jnp.stack([real_part, imag_part]) * scale).astype(jnp.bfloat16)


def solution(mesh):
    placed = (P("chan", ("hours", "freq"), None),)
    return jax.shard_map(
        local,
        mesh=mesh,
        in_specs=placed,
        out_specs=P(None, ("hours", "freq"), None, "chan"),
        check_vma=False,
    )
```

profile of v0, /device:TPU:0, one launch (start us, length us, event | category | flops | bytes accessed | tf_op | source)
XLA Modules:
  0.0 168.4 jit_solution(10404083622506896489)
XLA Ops:
  0.0 0.0 copy-start
  0.1 2.1 %cosine_multiply_fusion = (f32[1024,128]{1,0:T(8,128)S(1)}, f32[1024,128]{1,0:T(8,128)S(1)}) fusion(s32[128]{0:T(128)S(1)} %iota_add_fusion, f32[1024]{0:T(1024)S(1)} %multiply_subtract_fusion), kind=kLoop, calls=%fused_computation.36 | loop fusion | flops 2228224 | bytes 1053184 | tf_op jit(solution)/shard_map/mul | solution.py:39
  2.2 0.0 copy-done
  2.2 0.8 fusion.7
  3.0 0.1 convert_element_type.44
  3.1 2.7 %copy.14 = bf16[2,128,2,576]{3,2,0,1:T(2,128)(2,1)} copy(bf16[2,128,2,576]{1,0,3,2:T(2,128)(2,1)S(1)} %convert_element_type.44) | data formatting | bytes 1179648 | tf_op jit(solution)/shard_map/convert_element_type | solution.py:63
  5.8 7.3 %all-to-all-start = ((bf16[2,128,2,576]{3,2,0,1:T(2,128)(2,1)}), bf16[2,128,2,576]{3,2,0,1:T(2,128)(2,1)S(1)}, u32[]{:S(2)}, u32[]{:S(2)}) async-start(bf16[2,128,2,576]{3,2,0,1:T(2,128)(2,1)} %copy.14), calls=%async_computation | async-start | bytes 1310720 | tf_op jit(solution)/shard_map/all_to_all | solution.py:64
  13.1 17.3 %all-to-all-done = bf16[2,128,2,576]{3,2,0,1:T(2,128)(2,1)S(1)} async-done(((bf16[2,128,2,576]{3,2,0,1:T(2,128)(2,1)}), bf16[2,128,2,576]{3,2,0,1:T(2,128)(2,1)S(1)}, u32[]{:S(2)}, u32[]{:S(2)}) %all-to-all-start) | async-done | bytes 589856 | tf_op jit(solution)/shard_map/all_to_all | solution.py:64
  30.4 0.1 copy.15
  30.5 0.7 copy.16
  31.1 0.5 all_to_all.16
  31.7 3.4 %collective-permute-start = (bf16[2,2,16,576]{3,2,1,0:T(8,128)(2,1)S(1)}, bf16[2,2,16,576]{3,2,1,0:T(8,128)(2,1)S(1)}, u32[]{:S(2)}, u32[]{:S(2)}) collective-permute-start(bf16[2,2,16,576]{3,2,1,0:T(8,128)(2,1)S(1)} %get-tuple-element.7), channel_id=1, source_target_pairs={{0,1},{1,2},{2,3},{3,4},{4,5},{5,6},{6,7},{8,9},{9,10},{10,11},{11... | collective-permute-start | bytes 221192 | tf_op jit(solution)/shard_map/ppermute | solution.py:18
  35.1 1.3 collective-permute-start.1
  36.4 0.7 collective-permute-done
  37.1 4.3 %collective-permute-done.1 = bf16[2,2,16,576]{3,2,1,0:T(8,128)(2,1)S(1)} collective-permute-done((bf16[2,2,16,576]{3,2,1,0:T(8,128)(2,1)S(1)}, bf16[2,2,16,576]{3,2,1,0:T(8,128)(2,1)S(1)}, u32[]{:S(2)}, u32[]{:S(2)}) %collective-permute-start.1) | collective-permute-done | bytes 73760 | tf_op jit(solution)/shard_map/ppermute | solution.py:20
  41.4 0.2 maximum_convert_fusion
  41.6 0.1 fusion.11
  41.7 0.3 fusion.15
  42.0 0.1 fusion.6
  42.1 0.1 collective-permute-start.2
  42.3 0.1 fusion.37
  42.4 1.9 %collective-permute-done.2 = bf16[2,16,16,576]{3,2,1,0:T(8,128)(2,1)S(1)} collective-permute-done((bf16[2,16,16,576]{3,2,1,0:T(8,128)(2,1)S(1)}, bf16[2,16,16,576]{3,2,1,0:T(8,128)(2,1)S(1)}, u32[]{:S(2)}, u32[]{:S(2)}) %collective-permute-start.2) | collective-permute-done | bytes 589856 | tf_op jit(solution)/shard_map/ppermute | solution.py:30
  44.3 0.2 pad_maximum_fusion
  44.5 1.8 %gather_fusion = bf16[2,2,16,16,576]{4,3,2,1,0:T(8,128)(2,1)} fusion(bf16[2,2,16,16,576]{4,3,2,1,0:T(8,128)(2,1)S(1)} %pad_maximum_fusion, s32[1024]{0:T(1024)S(1)} %pad_clamp_fusion), kind=kCustom, calls=%fused_computation | custom fusion | bytes 2359304 | tf_op jit(solution)/shard_map/jit(_take)/gather | solution.py:78
  46.3 1.5 select_bitcast_fusion
  47.8 2.4 %copy.17 = bf16[2,16,16,2,576]{4,3,2,1,0:T(2,128)(2,1)} copy(bf16[2,16,16,2,576]{4,2,1,0,3:T(8,128)(2,1)S(1)} %select_bitcast_fusion) | data formatting | bytes 2359296 | tf_op jit(solution)/shard_map/jit(_take)/select_n | solution.py:78
  50.2 1.0 fusion.31
  51.2 3.1 %reshape.85 = bf16[2,16,16,1152]{3,2,1,0:T(8,128)(2,1)S(1)} reshape(bf16[2,16,16,2,576]{4,3,2,1,0:T(2,128)(2,1)} %copy.17) | data formatting | bytes 2359296 | tf_op jit(solution)/shard_map/reshape | solution.py:79
  54.2 1.5 copy.19
  55.7 2.0 %squeeze.18 = bf16[16,16,1152]{2,1,0:T(8,128)(2,1)S(1)} reshape(bf16[1,16,16,2,576]{4,3,2,1,0:T(2,128)(2,1)} %copy.19) | data formatting | bytes 1179648 | tf_op jit(solution)/shard_map/squeeze | solution.py:87
  57.8 2.6 %copy.18 = bf16[1,16,16,2,576]{4,3,2,1,0:T(2,128)(2,1)} copy(bf16[1,16,16,2,576]{4,2,1,0,3:T(8,128)(2,1)} %get-tuple-element.6) | data formatting | bytes 1179648 | tf_op jit(solution)/shard_map/slice | solution.py:84
  60.4 2.0 %squeeze.16 = bf16[16,16,1152]{2,1,0:T(8,128)(2,1)S(1)} reshape(bf16[1,16,16,2,576]{4,3,2,1,0:T(2,128)(2,1)} %copy.18) | data formatting | bytes 1179648 | tf_op jit(solution)/shard_map/squeeze | solution.py:84
  62.4 16.5 %convolution_bitcast_fusion = f32[1,16,1152,576]{2,3,1,0:T(8,128)} fusion(bf16[2,16,16,1152]{3,2,1,0:T(8,128)(2,1)S(1)} %reshape.85, bf16[2,16,16,576]{3,2,1,0:T(8,128)(2,1)S(1)} %fusion.6), kind=kOutput, calls=%fused_computation.4 | convolution fusion | flops 679477248 | bytes 44236800 | tf_op jit(solution)/shard_map/pkwb,pkwa->kba/dot_general | solution.py:82
  78.9 17.6 %fusion.25 = f32[16,1152,576]{1,2,0:T(8,128)} fusion(bf16[16,16,1152]{2,1,0:T(8,128)(2,1)S(1)} %squeeze.16, bf16[2,16,16,576]{3,2,1,0:T(8,128)(2,1)S(1)} %fusion.6), kind=kOutput, calls=%fused_computation.42 | convolution fusion | flops 339738624 | bytes 43384832 | tf_op jit(solution)/shard_map/kwb,kwa->kba/dot_general | solution.py:83
  96.5 30.7 %subtract_bitcast_fusion = f32[1,16,1152,576]{2,3,1,0:T(8,128)} fusion(f32[16,1152,576]{1,2,0:T(8,128)} %fusion.25, bf16[16,16,1152]{2,1,0:T(8,128)(2,1)S(1)} %squeeze.18, bf16[2,16,16,576]{3,2,1,0:T(8,128)(2,1)S(1)} %fusion.6), kind=kOutput, calls=%fused_computation.3 | convolution fusion | flops 350355456 | bytes 85852160 | tf_op jit(solution)/shard_map/kwb,kwa->kba/dot_general | solution.py:86
  127.2 0.0 copy-start.1
  127.2 41.0 %fusion = bf16[2,16,1152,576]{2,3,1,0:T(8,128)(2,1)} fusion(f32[1,16,1152,576]{2,3,1,0:T(8,128)} %subtract_bitcast_fusion, f32[1,16,1152,576]{2,3,1,0:T(8,128)} %convolution_bitcast_fusion), kind=kLoop, calls=%fused_computation.2 | loop fusion | flops 63700992 | bytes 127401984 | tf_op jit(solution)/shard_map/convert_element_type | solution.py:89
  168.2 0.0 copy-done.1
  (7 shorter events, 0.1 us)
Async XLA Ops:
  0.0 2.2 %copy-start = (bf16[576,2,1024]{2,1,0:T(2,128)(2,1)S(1)}, bf16[576,2,1024]{2,1,0:T(2,128)(2,1)}, u32[]{:S(2)}) copy-start(bf16[576,2,1024]{2,1,0:T(2,128)(2,1)} %param.1) | copy-start | bytes 7077892
  5.8 24.6 %all-to-all-start = ((bf16[2,128,2,576]{3,2,0,1:T(2,128)(2,1)}), bf16[2,128,2,576]{3,2,0,1:T(2,128)(2,1)S(1)}, u32[]{:S(2)}, u32[]{:S(2)}) async-start(bf16[2,128,2,576]{3,2,0,1:T(2,128)(2,1)} %copy.14), calls=%async_computation | async-start | bytes 1310720 | tf_op jit(solution)/shard_map/all_to_all | solution.py:64
  31.7 5.4 %collective-permute-start = (bf16[2,2,16,576]{3,2,1,0:T(8,128)(2,1)S(1)}, bf16[2,2,16,576]{3,2,1,0:T(8,128)(2,1)S(1)}, u32[]{:S(2)}, u32[]{:S(2)}) collective-permute-start(bf16[2,2,16,576]{3,2,1,0:T(8,128)(2,1)S(1)} %get-tuple-element.7), channel_id=1, source_target_pairs={{0,1},{1,2},{2,3},{3,4},{4,5},{5,6},{6,7},{8,9},{9,10},{10,11},{11... | collective-permute-start | bytes 221192 | tf_op jit(solution)/shard_map/ppermute | solution.py:18
  35.1 6.3 %collective-permute-start.1 = (bf16[2,2,16,576]{3,2,1,0:T(8,128)(2,1)S(1)}, bf16[2,2,16,576]{3,2,1,0:T(8,128)(2,1)S(1)}, u32[]{:S(2)}, u32[]{:S(2)}) collective-permute-start(bf16[2,2,16,576]{3,2,1,0:T(8,128)(2,1)S(1)} %get-tuple-element.8), channel_id=1, source_target_pairs={{1,0},{2,1},{3,2},{4,3},{5,4},{6,5},{7,6},{9,8},{10,9},{11,10},{12... | collective-permute-start | bytes 221192 | tf_op jit(solution)/shard_map/ppermute | solution.py:20
  42.1 2.2 %collective-permute-start.2 = (bf16[2,16,16,576]{3,2,1,0:T(8,128)(2,1)S(1)}, bf16[2,16,16,576]{3,2,1,0:T(8,128)(2,1)S(1)}, u32[]{:S(2)}, u32[]{:S(2)}) collective-permute-start(bf16[2,16,16,576]{3,2,1,0:T(8,128)(2,1)S(1)} %fusion.6), channel_id=1, source_target_pairs={{0,8},{8,0},{1,9},{9,1},{2,10},{10,2},{3,11},{11,3},{4,12},{12,4},... | collective-permute-start | bytes 1769480 | tf_op jit(solution)/shard_map/ppermute | solution.py:30
  127.2 41.0 %copy-start.1 = (bf16[576,2,1024]{2,1,0:T(2,128)(2,1)S(1)}, bf16[576,2,1024]{2,1,0:T(2,128)(2,1)}, u32[]{:S(2)}) copy-start(bf16[576,2,1024]{2,1,0:T(2,128)(2,1)} %param.1) | copy-start | bytes 7077892
where the time goes:
time: 169 us; the launch traced here: 168 us
  matrix products  65.5 us (39%)
  other arithmetic  45.8 us (27%)
  waiting for transfers between devices  24.2 us (14%)
  local copies, waits for them, and re-layouts  20.4 us (12%)
  starting transfers between devices  12 us (7%)
    convert_element_type x1, other arithmetic, local(): return (jnp.stack([real_part, imag_part]) * scale).astype(jnp.bfloat16)  41 us
    dot_general x1, matrix products, local(): jnp.einsum('kwb,kwa->kba', every[1], whitened[0], preferred_element_type=...  30.7 us
    dot_general x1, matrix products, local(): jnp.einsum('kwb,kwa->kba', every[0], whitened[1], preferred_element_type=...  17.6 us
    all_to_all x1, waiting for transfers between devices, local(): lax.all_to_all(spectrum, 'freq', split_axis=1, concat_axis=2, tiled=True)  17.3 us
    dot_general x1, matrix products, local(): jnp.einsum('pkwb,pkwa->kba', every, whitened, preferred_element_type=jnp....  16.5 us
    all_to_all x1, starting transfers between devices, local(): lax.all_to_all(spectrum, 'freq', split_axis=1, concat_axis=2, tiled=True)  7.28 us
    ppermute x1, waiting for transfers between devices, padded_2(): lax.ppermute(head, axis, [((i + 1) % count, i) for i in range(ends)])  4.3 us
  transfers between devices with their start and end apart: 4, of which 4 were waited for; matrix products, arithmetic and copies ran while one was open for 0% of the time, Pallas kernels for 0%

commit v1 on v0

--- a/solution.py
+++ b/solution.py
@@ -5,6 +5,28 @@
 from jax.sharding import PartitionSpec as P
 
 BINS = 128
+
+
+def cut_along(x, dim, size):
+    before, after = (x.shape[:dim], x.shape[dim + 1 :])
+    return jnp.moveaxis(x.reshape(*before, size, -1, *after), dim, 0)
+
+
+def in_order(blocks, dim):
+    dims = list(blocks.shape[1:])
+    dims[dim] *= blocks.shape[0]
+    return jnp.moveaxis(blocks, 0, dim).reshape(dims)
+
+
+def rotated_exchange(x, axis, split_dim, concat_dim):
+    length, index = (lax.axis_size(axis), lax.axis_index(axis))
+    tiles = cut_along(x, split_dim, length)
+    outs = [tiles[index]]
+    for step in range(1, length):
+        sent = tiles[(index + step) % length]
+        outs.append(lax.ppermute(sent, axis, [(i, (i + step) % length) for i in range(length)]))
+    tiles = jnp.stack(outs)[(index - jnp.arange(length)) % length]
+    return in_order(tiles, concat_dim)
 
 
 def padded_2(cells, sides, width):
@@ -61,7 +83,7 @@
     table = bin_table(length, BINS)
     spectrum = jnp.einsum("cws,sj->jwc", samples, table, preferred_element_type=jnp.float32)
     spectrum = spectrum.reshape(2, BINS, local_windows, local_channels).astype(jnp.bfloat16)
-    arrived = lax.all_to_all(spectrum, "freq", split_axis=1, concat_axis=2, tiled=True)
+    arrived = rotated_exchange(spectrum, "freq", 1, 2)
     rimmed = padded_2(arrived, (("freq", 1),), 2)
     whitened = whiten(rimmed, lax.axis_index("freq") * arrived.shape[1], BINS)
     local_bins = whitened.shape[1]

time: 169 us -> 162 us (0.959)
  waiting for transfers between devices: 24.2 us -> 11.4 us
  starting transfers between devices: 12 us -> 19.7 us
  local copies, waits for them, and re-layouts: 20.4 us -> 18.6 us
    all_to_all x1 -> x0, waiting for transfers between devices: 17.3 us -> none  [local(): lax.all_to_all(spectrum, 'freq', split_axis=1, concat_axis=2, tiled=True)]
    ppermute x0 -> x7, starting transfers between devices: none -> 14.1 us  [rotated_exchange(): lax.ppermute(sent, axis, [(i, (i + step) % length) for i in range(length)])]
    all_to_all x1 -> x0, starting transfers between devices: 7.28 us -> none  [local(): lax.all_to_all(spectrum, 'freq', split_axis=1, concat_axis=2, tiled=True)]
    ppermute x0 -> x7, waiting for transfers between devices: none -> 4.5 us  [rotated_exchange(): lax.ppermute(sent, axis, [(i, (i + step) % length) for i in range(length)])]
    convert_element_type x2 -> x1, local copies, waits for them, and re-layouts: 2.82 us -> 0.29 us  [local(): spectrum.reshape(2, BINS, local_windows, local_channels)]
  transfers between devices with their start and end apart: 4 -> 10, of which waited for: 4 -> 6; matrix products, arithmetic and copies ran while one was open for 0% -> 0% of each run, Pallas kernels for 0% -> 0%
where the time goes in v1:
time: 162 us
  matrix products  65.5 us (40%)
  other arithmetic  45.9 us (28%)
  starting transfers between devices  19.7 us (12%)
  local copies, waits for them, and re-layouts  18.6 us (11%)
  waiting for transfers between devices  11.4 us (7%)
    convert_element_type x1, other arithmetic, local(): return (jnp.stack([real_part, imag_part]) * scale).astype(jnp.bfloat16)  41 us
    dot_general x1, matrix products, local(): jnp.einsum('kwb,kwa->kba', every[1], whitened[0], preferred_element_type=...  30.7 us
    dot_general x1, matrix products, local(): jnp.einsum('kwb,kwa->kba', every[0], whitened[1], preferred_element_type=...  17.6 us
    dot_general x1, matrix products, local(): jnp.einsum('pkwb,pkwa->kba', every, whitened, preferred_element_type=jnp....  16.5 us
    ppermute x7, starting transfers between devices, rotated_exchange(): lax.ppermute(sent, axis, [(i, (i + step) % length) for i in range(length)])  14.1 us
    ppermute x7, waiting for transfers between devices, rotated_exchange(): lax.ppermute(sent, axis, [(i, (i + step) % length) for i in range(length)])  4.5 us
    ppermute x1, waiting for transfers between devices, padded_2(): lax.ppermute(head, axis, [((i + 1) % count, i) for i in range(ends)])  4.3 us
    ppermute x1, starting transfers between devices, padded_2(): lax.ppermute(tail, axis, [(i, (i + 1) % count) for i in range(ends)])  4.22 us
  transfers between devices with their start and end apart: 10, of which 6 were waited for; matrix products, arithmetic and copies ran while one was open for 0% of the time, Pallas kernels for 0%

profile of v1, /device:TPU:0, one launch (start us, length us, event | category | flops | bytes accessed | tf_op | source)
XLA Modules:
  0.0 161.5 jit_solution(14397242577792959609)
XLA Ops:
  0.0 0.0 copy-start
  0.1 2.1 %cosine_multiply_fusion = (f32[1024,128]{1,0:T(8,128)S(1)}, f32[1024,128]{1,0:T(8,128)S(1)}) fusion(s32[128]{0:T(128)S(1)} %iota_add_fusion, f32[1024]{0:T(1024)S(1)} %multiply_subtract_fusion), kind=kLoop, calls=%fused_computation.37 | loop fusion | flops 2228224 | bytes 1053184 | tf_op jit(solution)/shard_map/mul | solution.py:61
  2.2 0.0 copy-done
  2.2 0.8 fusion.7
  3.0 0.3 copy.5
  3.3 0.1 constant_dynamic-slice_fusion
  3.4 3.0 %collective-permute-start = (bf16[2,16,2,576]{3,1,2,0:T(8,128)(2,1)S(1)}, bf16[2,16,2,576]{3,1,2,0:T(8,128)(2,1)S(1)}, u32[]{:S(2)}, u32[]{:S(2)}) collective-permute-start(bf16[2,16,2,576]{3,1,2,0:T(8,128)(2,1)S(1)} %bitcast.84), channel_id=1, source_target_pairs={{0,1},{1,2},{2,3},{3,4},{4,5},{5,6},{6,7},{7,0},{8,9},{9,10},{10,1... | collective-permute-start | bytes 221192 | tf_op jit(solution)/shard_map/ppermute | solution.py:27
  6.5 1.6 %collective-permute-start.1 = (bf16[2,16,2,576]{3,1,2,0:T(8,128)(2,1)S(1)}, bf16[2,16,2,576]{3,1,2,0:T(8,128)(2,1)S(1)}, u32[]{:S(2)}, u32[]{:S(2)}) collective-permute-start(bf16[2,16,2,576]{3,1,2,0:T(8,128)(2,1)S(1)} %bitcast.83), channel_id=1, source_target_pairs={{0,2},{1,3},{2,4},{3,5},{4,6},{5,7},{6,0},{7,1},{8,10},{9,11},{10,... | collective-permute-start | bytes 221192 | tf_op jit(solution)/shard_map/ppermute | solution.py:27
  8.1 2.6 %collective-permute-start.2 = (bf16[2,16,2,576]{3,1,2,0:T(8,128)(2,1)S(1)}, bf16[2,16,2,576]{3,1,2,0:T(8,128)(2,1)S(1)}, u32[]{:S(2)}, u32[]{:S(2)}) collective-permute-start(bf16[2,16,2,576]{3,1,2,0:T(8,128)(2,1)S(1)} %bitcast.81), channel_id=1, source_target_pairs={{0,3},{1,4},{2,5},{3,6},{4,7},{5,0},{6,1},{7,2},{8,11},{9,12},{10,... | collective-permute-start | bytes 221192 | tf_op jit(solution)/shard_map/ppermute | solution.py:27
  10.7 1.3 collective-permute-start.3
  12.0 2.7 %collective-permute-start.4 = (bf16[2,16,2,576]{3,1,2,0:T(8,128)(2,1)S(1)}, bf16[2,16,2,576]{3,1,2,0:T(8,128)(2,1)S(1)}, u32[]{:S(2)}, u32[]{:S(2)}) collective-permute-start(bf16[2,16,2,576]{3,1,2,0:T(8,128)(2,1)S(1)} %bitcast.79), channel_id=1, source_target_pairs={{0,5},{1,6},{2,7},{3,0},{4,1},{5,2},{6,3},{7,4},{8,13},{9,14},{10,... | collective-permute-start | bytes 221192 | tf_op jit(solution)/shard_map/ppermute | solution.py:27
  14.8 0.0 collective-permute-done
  14.8 1.4 collective-permute-start.5
  16.2 0.0 collective-permute-done.1
  16.2 1.5 collective-permute-start.6
  17.7 1.5 collective-permute-done.2
  19.2 0.7 collective-permute-done.3
  19.9 0.0 collective-permute-done.4
  19.9 2.3 %collective-permute-done.5 = bf16[2,16,2,576]{3,1,2,0:T(8,128)(2,1)S(1)} collective-permute-done((bf16[2,16,2,576]{3,1,2,0:T(8,128)(2,1)S(1)}, bf16[2,16,2,576]{3,1,2,0:T(8,128)(2,1)S(1)}, u32[]{:S(2)}, u32[]{:S(2)}) %collective-permute-start.5) | collective-permute-done | bytes 73760 | tf_op jit(solution)/shard_map/ppermute | solution.py:27
  22.3 0.0 collective-permute-done.6
  22.3 0.7 gather_fusion
  23.0 0.5 copy.14
  23.5 0.5 reshape.154
  24.0 4.2 %collective-permute-start.7 = (bf16[2,2,16,576]{3,2,1,0:T(8,128)(2,1)S(1)}, bf16[2,2,16,576]{3,2,1,0:T(8,128)(2,1)S(1)}, u32[]{:S(2)}, u32[]{:S(2)}) collective-permute-start(bf16[2,2,16,576]{3,2,1,0:T(8,128)(2,1)S(1)} %get-tuple-element.7), channel_id=1, source_target_pairs={{0,1},{1,2},{2,3},{3,4},{4,5},{5,6},{6,7},{8,9},{9,10},{10,11},{11... | collective-permute-start | bytes 221192 | tf_op jit(solution)/shard_map/ppermute | solution.py:40
  28.2 1.3 collective-permute-start.8
  29.6 0.7 collective-permute-done.7
  30.3 4.3 %collective-permute-done.8 = bf16[2,2,16,576]{3,2,1,0:T(8,128)(2,1)S(1)} collective-permute-done((bf16[2,2,16,576]{3,2,1,0:T(8,128)(2,1)S(1)}, bf16[2,2,16,576]{3,2,1,0:T(8,128)(2,1)S(1)}, u32[]{:S(2)}, u32[]{:S(2)}) %collective-permute-start.8) | collective-permute-done | bytes 73760 | tf_op jit(solution)/shard_map/ppermute | solution.py:42
  34.6 0.2 maximum_convert_fusion
  34.7 0.1 fusion.11
  34.8 0.3 fusion.15
  35.2 0.1 fusion.6
  35.3 0.1 collective-permute-start.9
  35.5 0.1 fusion.39
  35.6 1.9 %collective-permute-done.9 = bf16[2,16,16,576]{3,2,1,0:T(8,128)(2,1)S(1)} collective-permute-done((bf16[2,16,16,576]{3,2,1,0:T(8,128)(2,1)S(1)}, bf16[2,16,16,576]{3,2,1,0:T(8,128)(2,1)S(1)}, u32[]{:S(2)}, u32[]{:S(2)}) %collective-permute-start.9) | collective-permute-done | bytes 589856 | tf_op jit(solution)/shard_map/ppermute | solution.py:52
  37.5 0.2 pad_maximum_fusion
  37.7 1.8 %gather_fusion.1 = bf16[2,2,16,16,576]{4,3,2,1,0:T(8,128)(2,1)} fusion(bf16[2,2,16,16,576]{4,3,2,1,0:T(8,128)(2,1)S(1)} %pad_maximum_fusion, s32[1024]{0:T(1024)S(1)} %pad_clamp_fusion), kind=kCustom, calls=%fused_computation.1 | custom fusion | bytes 2359304 | tf_op jit(solution)/shard_map/jit(_take)/gather | solution.py:100
  39.5 1.5 select_bitcast_fusion
  41.0 2.4 %copy.15 = bf16[2,16,16,2,576]{4,3,2,1,0:T(2,128)(2,1)} copy(bf16[2,16,16,2,576]{4,2,1,0,3:T(8,128)(2,1)S(1)} %select_bitcast_fusion) | data formatting | bytes 2359296 | tf_op jit(solution)/shard_map/jit(_take)/select_n | solution.py:100
  43.4 1.0 fusion.33
  44.3 3.1 %reshape.177 = bf16[2,16,16,1152]{3,2,1,0:T(8,128)(2,1)S(1)} reshape(bf16[2,16,16,2,576]{4,3,2,1,0:T(2,128)(2,1)} %copy.15) | data formatting | bytes 2359296 | tf_op jit(solution)/shard_map/reshape | solution.py:101
  47.4 1.5 copy.19
  48.9 2.0 %squeeze.46 = bf16[16,16,1152]{2,1,0:T(8,128)(2,1)S(1)} reshape(bf16[1,16,16,2,576]{4,3,2,1,0:T(2,128)(2,1)} %copy.19) | data formatting | bytes 1179648 | tf_op jit(solution)/shard_map/squeeze | solution.py:109
  51.0 2.6 %copy.18 = bf16[1,16,16,2,576]{4,3,2,1,0:T(2,128)(2,1)} copy(bf16[1,16,16,2,576]{4,2,1,0,3:T(8,128)(2,1)} %get-tuple-element.6) | data formatting | bytes 1179648 | tf_op jit(solution)/shard_map/slice | solution.py:106
  53.6 2.0 %squeeze.44 = bf16[16,16,1152]{2,1,0:T(8,128)(2,1)S(1)} reshape(bf16[1,16,16,2,576]{4,3,2,1,0:T(2,128)(2,1)} %copy.18) | data formatting | bytes 1179648 | tf_op jit(solution)/shard_map/squeeze | solution.py:106
  55.6 16.5 %convolution_bitcast_fusion = f32[1,16,1152,576]{2,3,1,0:T(8,128)} fusion(bf16[2,16,16,1152]{3,2,1,0:T(8,128)(2,1)S(1)} %reshape.177, bf16[2,16,16,576]{3,2,1,0:T(8,128)(2,1)S(1)} %fusion.6), kind=kOutput, calls=%fused_computation.5 | convolution fusion | flops 679477248 | bytes 44236800 | tf_op jit(solution)/shard_map/pkwb,pkwa->kba/dot_general | solution.py:104
  72.1 17.6 %fusion.25 = f32[16,1152,576]{1,2,0:T(8,128)} fusion(bf16[16,16,1152]{2,1,0:T(8,128)(2,1)S(1)} %squeeze.44, bf16[2,16,16,576]{3,2,1,0:T(8,128)(2,1)S(1)} %fusion.6), kind=kOutput, calls=%fused_computation.43 | convolution fusion | flops 339738624 | bytes 43384832 | tf_op jit(solution)/shard_map/kwb,kwa->kba/dot_general | solution.py:105
  89.7 30.7 %subtract_bitcast_fusion = f32[1,16,1152,576]{2,3,1,0:T(8,128)} fusion(f32[16,1152,576]{1,2,0:T(8,128)} %fusion.25, bf16[16,16,1152]{2,1,0:T(8,128)(2,1)S(1)} %squeeze.46, bf16[2,16,16,576]{3,2,1,0:T(8,128)(2,1)S(1)} %fusion.6), kind=kOutput, calls=%fused_computation.4 | convolution fusion | flops 350355456 | bytes 85852160 | tf_op jit(solution)/shard_map/kwb,kwa->kba/dot_general | solution.py:108
  120.3 0.0 copy-start.1
  120.3 41.0 %fusion = bf16[2,16,1152,576]{2,3,1,0:T(8,128)(2,1)} fusion(f32[1,16,1152,576]{2,3,1,0:T(8,128)} %subtract_bitcast_fusion, f32[1,16,1152,576]{2,3,1,0:T(8,128)} %convolution_bitcast_fusion), kind=kLoop, calls=%fused_computation.3 | loop fusion | flops 63700992 | bytes 127401984 | tf_op jit(solution)/shard_map/convert_element_type | solution.py:111
  161.4 0.0 copy-done.1
  (24 shorter events, 0.3 us)
Async XLA Ops:
  0.0 2.2 %copy-start = (bf16[576,2,1024]{2,1,0:T(2,128)(2,1)S(1)}, bf16[576,2,1024]{2,1,0:T(2,128)(2,1)}, u32[]{:S(2)}) copy-start(bf16[576,2,1024]{2,1,0:T(2,128)(2,1)} %param.1) | copy-start | bytes 7077892
  3.4 11.4 %collective-permute-start = (bf16[2,16,2,576]{3,1,2,0:T(8,128)(2,1)S(1)}, bf16[2,16,2,576]{3,1,2,0:T(8,128)(2,1)S(1)}, u32[]{:S(2)}, u32[]{:S(2)}) collective-permute-start(bf16[2,16,2,576]{3,1,2,0:T(8,128)(2,1)S(1)} %bitcast.84), channel_id=1, source_target_pairs={{0,1},{1,2},{2,3},{3,4},{4,5},{5,6},{6,7},{7,0},{8,9},{9,10},{10,1... | collective-permute-start | bytes 221192 | tf_op jit(solution)/shard_map/ppermute | solution.py:27
  6.5 9.8 %collective-permute-start.1 = (bf16[2,16,2,576]{3,1,2,0:T(8,128)(2,1)S(1)}, bf16[2,16,2,576]{3,1,2,0:T(8,128)(2,1)S(1)}, u32[]{:S(2)}, u32[]{:S(2)}) collective-permute-start(bf16[2,16,2,576]{3,1,2,0:T(8,128)(2,1)S(1)} %bitcast.83), channel_id=1, source_target_pairs={{0,2},{1,3},{2,4},{3,5},{4,6},{5,7},{6,0},{7,1},{8,10},{9,11},{10,... | collective-permute-start | bytes 221192 | tf_op jit(solution)/shard_map/ppermute | solution.py:27
  8.1 11.1 %collective-permute-start.2 = (bf16[2,16,2,576]{3,1,2,0:T(8,128)(2,1)S(1)}, bf16[2,16,2,576]{3,1,2,0:T(8,128)(2,1)S(1)}, u32[]{:S(2)}, u32[]{:S(2)}) collective-permute-start(bf16[2,16,2,576]{3,1,2,0:T(8,128)(2,1)S(1)} %bitcast.81), channel_id=1, source_target_pairs={{0,3},{1,4},{2,5},{3,6},{4,7},{5,0},{6,1},{7,2},{8,11},{9,12},{10,... | collective-permute-start | bytes 221192 | tf_op jit(solution)/shard_map/ppermute | solution.py:27
  10.7 9.2 %collective-permute-start.3 = (bf16[2,16,2,576]{3,1,2,0:T(8,128)(2,1)S(1)}, bf16[2,16,2,576]{3,1,2,0:T(8,128)(2,1)S(1)}, u32[]{:S(2)}, u32[]{:S(2)}) collective-permute-start(bf16[2,16,2,576]{3,1,2,0:T(8,128)(2,1)S(1)} %bitcast.80), channel_id=1, source_target_pairs={{0,4},{1,5},{2,6},{3,7},{4,0},{5,1},{6,2},{7,3},{8,12},{9,13},{10,... | collective-permute-start | bytes 221192 | tf_op jit(solution)/shard_map/ppermute | solution.py:27
  12.0 7.9 %collective-permute-start.4 = (bf16[2,16,2,576]{3,1,2,0:T(8,128)(2,1)S(1)}, bf16[2,16,2,576]{3,1,2,0:T(8,128)(2,1)S(1)}, u32[]{:S(2)}, u32[]{:S(2)}) collective-permute-start(bf16[2,16,2,576]{3,1,2,0:T(8,128)(2,1)S(1)} %bitcast.79), channel_id=1, source_target_pairs={{0,5},{1,6},{2,7},{3,0},{4,1},{5,2},{6,3},{7,4},{8,13},{9,14},{10,... | collective-permute-start | bytes 221192 | tf_op jit(solution)/shard_map/ppermute | solution.py:27
  14.8 7.5 %collective-permute-start.5 = (bf16[2,16,2,576]{3,1,2,0:T(8,128)(2,1)S(1)}, bf16[2,16,2,576]{3,1,2,0:T(8,128)(2,1)S(1)}, u32[]{:S(2)}, u32[]{:S(2)}) collective-permute-start(bf16[2,16,2,576]{3,1,2,0:T(8,128)(2,1)S(1)} %bitcast.85), channel_id=1, source_target_pairs={{0,6},{1,7},{2,0},{3,1},{4,2},{5,3},{6,4},{7,5},{8,14},{9,15},{10,... | collective-permute-start | bytes 221192 | tf_op jit(solution)/shard_map/ppermute | solution.py:27
  16.2 6.0 %collective-permute-start.6 = (bf16[2,16,2,576]{3,1,2,0:T(8,128)(2,1)S(1)}, bf16[2,16,2,576]{3,1,2,0:T(8,128)(2,1)S(1)}, u32[]{:S(2)}, u32[]{:S(2)}) collective-permute-start(bf16[2,16,2,576]{3,1,2,0:T(8,128)(2,1)S(1)} %bitcast.82), channel_id=1, source_target_pairs={{0,7},{1,0},{2,1},{3,2},{4,3},{5,4},{6,5},{7,6},{8,15},{9,8},{10,9... | collective-permute-start | bytes 221192 | tf_op jit(solution)/shard_map/ppermute | solution.py:27
  24.0 6.3 %collective-permute-start.7 = (bf16[2,2,16,576]{3,2,1,0:T(8,128)(2,1)S(1)}, bf16[2,2,16,576]{3,2,1,0:T(8,128)(2,1)S(1)}, u32[]{:S(2)}, u32[]{:S(2)}) collective-permute-start(bf16[2,2,16,576]{3,2,1,0:T(8,128)(2,1)S(1)} %get-tuple-element.7), channel_id=1, source_target_pairs={{0,1},{1,2},{2,3},{3,4},{4,5},{5,6},{6,7},{8,9},{9,10},{10,11},{11... | collective-permute-start | bytes 221192 | tf_op jit(solution)/shard_map/ppermute | solution.py:40
  28.2 6.3 %collective-permute-start.8 = (bf16[2,2,16,576]{3,2,1,0:T(8,128)(2,1)S(1)}, bf16[2,2,16,576]{3,2,1,0:T(8,128)(2,1)S(1)}, u32[]{:S(2)}, u32[]{:S(2)}) collective-permute-start(bf16[2,2,16,576]{3,2,1,0:T(8,128)(2,1)S(1)} %get-tuple-element.8), channel_id=1, source_target_pairs={{1,0},{2,1},{3,2},{4,3},{5,4},{6,5},{7,6},{9,8},{10,9},{11,10},{12... | collective-permute-start | bytes 221192 | tf_op jit(solution)/shard_map/ppermute | solution.py:42
  35.3 2.2 %collective-permute-start.9 = (bf16[2,16,16,576]{3,2,1,0:T(8,128)(2,1)S(1)}, bf16[2,16,16,576]{3,2,1,0:T(8,128)(2,1)S(1)}, u32[]{:S(2)}, u32[]{:S(2)}) collective-permute-start(bf16[2,16,16,576]{3,2,1,0:T(8,128)(2,1)S(1)} %fusion.6), channel_id=1, source_target_pairs={{0,8},{8,0},{1,9},{9,1},{2,10},{10,2},{3,11},{11,3},{4,12},{12,4},... | collective-permute-start | bytes 1769480 | tf_op jit(solution)/shard_map/ppermute | solution.py:52
  120.3 41.0 %copy-start.1 = (bf16[576,2,1024]{2,1,0:T(2,128)(2,1)S(1)}, bf16[576,2,1024]{2,1,0:T(2,128)(2,1)}, u32[]{:S(2)}) copy-start(bf16[576,2,1024]{2,1,0:T(2,128)(2,1)} %param.1) | copy-start | bytes 7077892
